TPU v7x, 32 devices: a whole 2x2x4 slice. The times are simulated.
32 devices in a mesh: node: 8 (over z, y), local: 4 (over x, core).
Axes of the slice: x: 2, y: 2, z: 4, core: 2. Of those that a mesh axis runs over, the one named last changes fastest.
Arguments:
- tokens: bfloat16 [256, 4096], P('node', 'local'), may hold values from -6 to 6
- node_ids: int32 [256, 4], P('node'), may hold values from 0 to 7, all different within a row; in each aligned block of 32 rows (0 to 31, 32 to 63, ...) at most 32 rows name the same one
- mix_weights: float32 [256, 4], P('node'), may hold values from 0.05 to 1
- w_gate: bfloat16 [8, 4096, 1024], P('node', 'local'), may hold values from -0.09375 to 0.09375
- w_up: bfloat16 [8, 4096, 1024], P('node', 'local'), may hold values from -0.09375 to 0.09375
- w_down: bfloat16 [8, 1024, 4096], P('node', None, 'local'), may hold values from -0.1875 to 0.1875
Outputs:
- mixed: bfloat16 [256, 4096], P('node', 'local')
Inputs may be any that keep to these rules, and one draw needn't show every extreme that they name: `node_ids`: each row names 4 different experts. Among the 32 tokens of one node (aligned blocks of rows), at most 32 name the same expert, and in every draw some expert is named by exactly 32 tokens of some node.
All inputs are finite; a program needn't handle non-finite values.
Results may differ from a plain program's by a relative error of at most 0.023.
Values may be sent and summed in bfloat16 or wider, within the bound.
A program may use at most 64 MiB of HBM per device.

v0:
```python
import jax
import jax.numpy as jnp
from jax import lax
from jax.sharding import PartitionSpec as P


def body(tokens, node_ids, mix_weights, w_gate, w_up, w_down):
    row_count, feat_width = tokens.shape
    pick_count = node_ids.shape[1]
    node_count = lax.axis_size("node")
    slot_cap = max(2, 2 * row_count * pick_count // node_count)
    slot_total = node_count * slot_cap
    flat_ids = node_ids.reshape(-1)
    hit_table = (flat_ids[:, None] == jnp.arange(node_count, dtype=jnp.int32)[None, :]).astype(
        jnp.int32
    )
    earlier = jnp.cumsum(hit_table, axis=0) - hit_table
    slot_rank = jnp.sum(earlier * hit_table, axis=1)
    position = flat_ids * slot_cap + slot_rank
    slot_table = jnp.arange(slot_total, dtype=jnp.int32)[:, None] == position[None, :]
    dispatch = jnp.any(slot_table.reshape(slot_total, row_count, pick_count), axis=2).astype(
        jnp.bfloat16
    )
    outbound = jnp.dot(dispatch, tokens, preferred_element_type=jnp.float32).astype(jnp.bfloat16)
    outbound = outbound.reshape(node_count, slot_cap, feat_width)
    inbound = lax.all_to_all(outbound, "node", split_axis=0, concat_axis=0, tiled=True)
    inbound = inbound.reshape(slot_total, feat_width)
    gate_part = jnp.dot(inbound, w_gate[0], preferred_element_type=jnp.float32)
    up_part = jnp.dot(inbound, w_up[0], preferred_element_type=jnp.float32)
    gate_whole, up_whole = (
        lax.psum(gate_part.astype(jnp.bfloat16), "local").astype(jnp.float32),
        lax.psum(up_part.astype(jnp.bfloat16), "local").astype(jnp.float32),
    )
    active = (jax.nn.silu(gate_whole) * up_whole).astype(jnp.bfloat16)
    result = jnp.dot(active, w_down[0], preferred_element_type=jnp.float32)
    expert_out = result.astype(jnp.bfloat16).reshape(node_count, slot_cap, feat_width)
    returned = lax.all_to_all(expert_out, "node", split_axis=0, concat_axis=0, tiled=True)
    returned = returned.reshape(slot_total, feat_width)
    weighting = slot_table.astype(jnp.float32) * mix_weights.reshape(-1)[None, :]
    combine = jnp.sum(weighting.reshape(slot_total, row_count, pick_count), axis=2)
    mixed = lax.dot_general(
        combine,
        returned.astype(jnp.float32),
        (((0,), (0,)), ((), ())),
        precision=lax.Precision.HIGHEST,
    )
    return mixed.astype(jnp.bfloat16)


def solution(mesh):
    return jax.shard_map(
        body,
        mesh=mesh,
        in_specs=(
            P("node", "local"),
            P("node", None),
            P("node", None),
            P("node", "local", None),
            P("node", "local", None),
            P("node", None, "local"),
        ),
        out_specs=P("node", "local"),
        check_vma=False,
    )
```

profile of v0, /device:TPU:0, one launch (start us, length us, event | category | flops | bytes accessed | tf_op | source)
XLA Modules:
  0.0 101.5 jit_solution(7903110153751656605)
XLA Ops:
  6.5 0.0 copy-start
  6.5 0.0 all-reduce.3.cloned.1.call-start
  6.5 0.9 copy.19
  7.5 0.1 eq.31
  7.6 0.1 fusion.23
  7.7 0.2 reduce_window_sum.11
  7.8 0.2 select_reduce_fusion.1
  8.0 0.1 reduce_sum.21
  8.1 0.1 copy.20
  8.2 0.7 multiply_add_fusion
  8.9 0.1 fusion.22
  9.0 1.2 %convolution_convert_fusion = bf16[256,1024]{1,0:T(8,128)(2,1)S(1)} fusion(pred[256,32]{0,1:T(8,128)(4,1)S(1)} %fusion.22, bf16[32,1024]{1,0:T(8,128)(2,1)} %param.6), kind=kOutput, calls=%fused_computation.11 | convolution fusion | flops 17039360 | bytes 598016 | tf_op jit(solution)/shard_map/dot_general | solution.py:24
  10.2 0.0 copy-start.2
  10.2 21.7 %all_to_all.10 = bf16[8,32,1024]{2,1,0:T(8,128)(2,1)S(1)} all-to-all(bf16[8,32,1024]{2,1,0:T(8,128)(2,1)S(1)} %bitcast.26), channel_id=1, replica_groups=mesh['node'=8,'local'=4] {'node'}, dimensions={0} | all-to-all | bytes 1048576 | tf_op jit(solution)/shard_map/all_to_all | solution.py:26
  31.9 0.0 copy-done
  31.9 1.5 %fusion.6 = bf16[256,1024]{1,0:T(8,128)(2,1)} fusion(bf16[256,1024]{1,0:T(8,128)(2,1)S(1)} %bitcast.27, bf16[1,1024,1024]{2,1,0:T(8,128)(2,1)S(1)} %copy-done), kind=kOutput, calls=%fused_computation.8 | convolution fusion | flops 537133056 | bytes 3145728 | tf_op jit(solution)/shard_map/dot_general | solution.py:28
  33.5 0.0 copy-done.2
  33.5 1.5 %fusion.9 = bf16[256,1024]{1,0:T(8,128)(2,1)} fusion(bf16[256,1024]{1,0:T(8,128)(2,1)S(1)} %bitcast.28, bf16[1,1024,1024]{2,1,0:T(8,128)(2,1)S(1)} %copy-done.2), kind=kOutput, calls=%fused_computation.9 | convolution fusion | flops 537133056 | bytes 3145728 | tf_op jit(solution)/shard_map/dot_general | solution.py:29
  35.0 0.0 all-reduce.3.cloned.1.call-update
  35.0 35.4 %all-reduce.3.cloned.1.call-done = (bf16[256,1024]{1,0:T(8,128)(2,1)}, bf16[256,1024]{1,0:T(8,128)(2,1)}) async-done(((bf16[256,1024]{1,0:T(8,128)(2,1)}, bf16[256,1024]{1,0:T(8,128)(2,1)}), (bf16[256,1024]{1,0:T(8,128)(2,1)}, bf16[256,1024]{1,0:T(8,128)(2,1)})) %all-reduce.3.cloned.1.call-update) | async-done | bytes 1048592 | tf_op jit(solution)/shard_map/psum | solution.py:32
  70.4 0.0 copy-start.1
  70.4 3.6 %fusion.12 = bf16[256,1024]{1,0:T(8,128)(2,1)} fusion(bf16[1,1024,1024]{2,1,0:T(8,128)(2,1)} %param.11, bf16[256,1024]{1,0:T(8,128)(2,1)} %get-tuple-element.5, bf16[256,1024]{1,0:T(8,128)(2,1)} %get-tuple-element.6), kind=kOutput, calls=%fused_computation.10 | convolution fusion | flops 539230208 | bytes 3670016 | tf_op jit(solution)/shard_map/dot_general | solution.py:35
  74.0 5.5 %all-to-all-start.1 = ((bf16[8,32,1024]{2,1,0:T(8,128)(2,1)}), bf16[8,32,1024]{2,1,0:T(8,128)(2,1)S(1)}, u32[]{:S(2)}, u32[]{:S(2)}) async-start(bf16[8,32,1024]{2,1,0:T(8,128)(2,1)} %bitcast.5), calls=%async_computation.1 | async-start | bytes 1048576 | tf_op jit(solution)/shard_map/all_to_all | solution.py:37
  79.5 0.0 copy-done.1
  79.5 0.1 select_reduce_fusion
  79.6 14.1 %all-to-all-done.1 = bf16[8,32,1024]{2,1,0:T(8,128)(2,1)S(1)} async-done(((bf16[8,32,1024]{2,1,0:T(8,128)(2,1)}), bf16[8,32,1024]{2,1,0:T(8,128)(2,1)S(1)}, u32[]{:S(2)}, u32[]{:S(2)}) %all-to-all-start.1) | async-done | bytes 524320 | tf_op jit(solution)/shard_map/all_to_all | solution.py:37
  93.7 1.0 convolution_convert_fusion.1
Async XLA Ops:
  6.5 25.4 %copy-start = (bf16[1,1024,1024]{2,1,0:T(8,128)(2,1)S(1)}, bf16[1,1024,1024]{2,1,0:T(8,128)(2,1)}, u32[]{:S(2)}) copy-start(bf16[1,1024,1024]{2,1,0:T(8,128)(2,1)} %param.9) | copy-start | bytes 6291460
  6.5 63.8 %all-reduce.3.cloned.1.call-start = ((), (), s32[]{:S(2)}) async-start(), calls=%async_computation.2 | async-start | bytes 2097152 | tf_op jit(solution)/shard_map/psum | solution.py:32
  10.2 23.3 %copy-start.2 = (bf16[1,1024,1024]{2,1,0:T(8,128)(2,1)S(1)}, bf16[1,1024,1024]{2,1,0:T(8,128)(2,1)}, u32[]{:S(2)}) copy-start(bf16[1,1024,1024]{2,1,0:T(8,128)(2,1)} %param.10) | copy-start | bytes 6291460
  70.4 9.1 %copy-start.1 = (f32[32,4]{0,1:T(4,128)S(1)}, f32[32,4]{0,1:T(4,128)}, u32[]{:S(2)}) copy-start(f32[32,4]{0,1:T(4,128)} %param.8) | copy-start | bytes 1540
  74.0 19.7 %all-to-all-start.1 = ((bf16[8,32,1024]{2,1,0:T(8,128)(2,1)}), bf16[8,32,1024]{2,1,0:T(8,128)(2,1)S(1)}, u32[]{:S(2)}, u32[]{:S(2)}) async-start(bf16[8,32,1024]{2,1,0:T(8,128)(2,1)} %bitcast.5), calls=%async_computation.1 | async-start | bytes 1048576 | tf_op jit(solution)/shard_map/all_to_all | solution.py:37
Sparse Core Ops, SparseCore 0:
  35.1 35.1 all-reduce.2
where the time goes:
time: 102 us; the launch traced here: 101 us
  waiting for transfers between devices  49.5 us (49%)
  blocking collectives  21.7 us (21%)
  between operations  13.5 us (13%)
  matrix products  8.79 us (9%)
  starting transfers between devices  5.52 us (5%)
  other arithmetic  1.31 us (1%)
  local copies, waits for them, and re-layouts  1.21 us (1%)
    psum x1, waiting for transfers between devices, body(): lax.psum(up_part.astype(jnp.bfloat16), 'local').astype(jnp.float32)  35.4 us
    all_to_all x1, blocking collectives, body(): lax.all_to_all(outbound, 'node', split_axis=0, concat_axis=0, tiled=True)  21.7 us
    all_to_all x1, waiting for transfers between devices, body(): lax.all_to_all(expert_out, 'node', split_axis=0, concat_axis=0, tiled=True)  14.1 us
    all_to_all x1, starting transfers between devices, body(): lax.all_to_all(expert_out, 'node', split_axis=0, concat_axis=0, tiled=True)  5.52 us
    dot_general x1, matrix products, body(): result = jnp.dot(active, w_down[0], preferred_element_type=jnp.float32)  3.57 us
  transfers between devices with their start and end apart: 2, of which 2 were waited for; matrix products, arithmetic and copies ran while one was open for 0% of the time, Pallas kernels for 0%

commit v1 on v0

--- a/solution.py
+++ b/solution.py
@@ -1,14 +1,256 @@
+import functools
+
 import jax
 import jax.numpy as jnp
 from jax import lax
+from jax.experimental import pallas as pl
+from jax.experimental.pallas import tpu as pltpu
 from jax.sharding import PartitionSpec as P
 
-
-def body(tokens, node_ids, mix_weights, w_gate, w_up, w_down):
+PAIR = 2
+LANES = 128
+F32 = jnp.float32
+BF16 = jnp.bfloat16
+
+
+def partner(index, step, count):
+    if count & (count - 1):
+        return lax.rem(index + step, count)
+    result, bit = 0, 1
+    while bit < count:
+        digit = lax.rem(index // bit, 2)
+        result = result + (1 - digit if step & bit else digit) * bit
+        bit *= 2
+    return result
+
+
+def fused_kernel(
+    tok, ids, mix, wg, wu, wd, out,
+    xbuf, vg, vu, vd, psend, precv, pown, xsend, xrecv, act, ysend, ykeep, yrecv,
+    zsend, zrecv, zown,
+    load_sem, a_zsend, a_ysend, a_recv, p_send, p_recv, x_send, x_recv,
+    t_send, t_recv, y_send, y_recv, z_send, z_recv,
+):
+    node_count, row_count, wide = xbuf.shape
+    feat = wide - LANES
+    groups = node_count // PAIR
+    rows = PAIR * row_count
+    hid = vg.shape[1]
+    half, quarter = hid // PAIR, hid // (PAIR * PAIR)
+    feat_out = vd.shape[1]
+    node, local = lax.axis_index("node"), lax.axis_index("local")
+    z, y = node // PAIR, lax.rem(node, PAIR)
+    x, c = local // PAIR, lax.rem(local, PAIR)
+    mine = c * PAIR + x
+
+    def at(zz, yy, xx, cc):
+        return {"node": zz * PAIR + yy, "local": xx * PAIR + cc}
+
+    y_peer, c_peer, x_peer = at(z, 1 - y, x, c), at(z, y, x, 1 - c), at(z, y, 1 - x, c)
+    d_peer = at(z, y, 1 - x, 1 - c)
+    z_peers = [at(partner(z, s, groups), y, x, c) for s in range(1, groups)]
+    planes = [partner(z, s, groups) for s in range(groups)]
+
+    def remote(src, dst, send, recv, device):
+        return pltpu.make_async_remote_copy(
+            src_ref=src, dst_ref=dst, send_sem=send, recv_sem=recv,
+            device_id=device, device_id_type=pl.DeviceIdType.MESH,
+        )
+
+    loads = [
+        pltpu.make_async_copy(tok, xbuf.at[node, :, pl.ds(0, feat)], load_sem.at[0]),
+        pltpu.make_async_copy(wg.at[0], vg, load_sem.at[1]),
+        pltpu.make_async_copy(wu.at[0], vu, load_sem.at[2]),
+        pltpu.make_async_copy(wd.at[0], vd, load_sem.at[3]),
+    ]
+    for load in loads:
+        load.start()
+    barrier = pltpu.get_barrier_semaphore()
+    peers = [y_peer, c_peer, x_peer, d_peer] + z_peers
+    for peer in peers:
+        pl.semaphore_signal(barrier, inc=1, device_id=peer, device_id_type=pl.DeviceIdType.MESH)
+
+    lane = lax.broadcasted_iota(jnp.int32, (row_count, LANES), 1)
+    weight = jnp.zeros((row_count, LANES), F32)
+    for k in range(ids.shape[1]):
+        expert = ids[:, k : k + 1]
+        weight += jnp.where(
+            (lane == expert) | (lane == expert + node_count), mix[:, k : k + 1], 0.0
+        )
+    head = weight.astype(BF16).astype(F32)
+    xbuf[node, :, feat:] = jnp.where(lane < node_count, head, weight - head).astype(BF16)
+    loads[0].wait()
+    pl.semaphore_wait(barrier, len(peers))
+
+    pending = []
+
+    def launch(copy):
+        copy.start()
+        pending.append(copy)
+
+    launch(remote(xbuf.at[node], xbuf.at[node], a_ysend.at[0], a_recv.at[node], y_peer))
+    for s in range(1, groups):
+        launch(
+            remote(xbuf.at[node], xbuf.at[node], a_zsend.at[s], a_recv.at[node], z_peers[s - 1])
+        )
+
+    def forward(s):
+        if not 0 < s < groups:
+            return
+        origin = planes[s] * PAIR + y
+        copy = remote(xbuf.at[origin], xbuf.at[origin], a_ysend.at[s], a_recv.at[origin], y_peer)
+        copy.wait_recv()
+        launch(copy)
+
+    def project(s):
+        origin = planes[s] * PAIR + 1 - y
+        remote(
+            xbuf.at[origin], xbuf.at[origin], a_ysend.at[s], a_recv.at[origin], y_peer
+        ).wait_recv()
+        if s == 0:
+            loads[1].wait()
+            loads[2].wait()
+        inputs = xbuf[pl.ds(planes[s] * PAIR, PAIR), :, :feat].reshape(rows, feat)
+        for target, first in ((psend, (1 - c) * half), (pown, c * half)):
+            for part in range(PAIR):
+                cols = pl.ds(pl.multiple_of(first + part * quarter, quarter), quarter)
+                for which, matrix in enumerate((vg, vu)):
+                    product = jnp.dot(inputs, matrix[:, cols], preferred_element_type=F32)
+                    start = (part * 2 + which) * quarter
+                    target[s, :, start : start + quarter] = product.astype(target.dtype)
+            if target is psend:
+                launch(remote(psend.at[s], precv.at[s], p_send.at[s], p_recv.at[s], c_peer))
+
+    def cross(s):
+        remote(psend.at[s], precv.at[s], p_send.at[s], p_recv.at[s], c_peer).wait_recv()
+        cols = pl.ds(pl.multiple_of((1 - x) * 2 * quarter, 2 * quarter), 2 * quarter)
+        xsend[s] = (pown[s, :, cols] + precv[s, :, cols].astype(F32)).astype(BF16)
+        launch(remote(xsend.at[s], xrecv.at[s], x_send.at[s], x_recv.at[s], x_peer))
+
+    def activate(s):
+        remote(xsend.at[s], xrecv.at[s], x_send.at[s], x_recv.at[s], x_peer).wait_recv()
+        cols = pl.ds(pl.multiple_of(x * 2 * quarter, 2 * quarter), 2 * quarter)
+        total = pown[s, :, cols] + precv[s, :, cols].astype(F32) + xrecv[s].astype(F32)
+        gate, up = total[:, :quarter], total[:, quarter:]
+        act[s, mine] = (gate / (1.0 + jnp.exp(-gate)) * up).astype(BF16)
+        for k, peer in enumerate((d_peer, x_peer, c_peer)):
+            launch(
+                remote(act.at[s, mine], act.at[s, mine], t_send.at[s, k], t_recv.at[s, mine], peer)
+            )
+
+    def down(s):
+        for k, (cc, xx) in enumerate(((1 - c, 1 - x), (c, 1 - x), (1 - c, x))):
+            slot = cc * PAIR + xx
+            remote(
+                act.at[s, slot], act.at[s, slot], t_send.at[s, k], t_recv.at[s, slot], d_peer
+            ).wait_recv()
+        if s == 0:
+            loads[3].wait()
+        hidden = jnp.concatenate([act[s, q] for q in range(PAIR * PAIR)], axis=1)
+        scales = xbuf[pl.ds(planes[s] * PAIR, PAIR), :, feat:].reshape(rows, LANES).astype(F32)
+        lanes = lax.broadcasted_iota(jnp.int32, (rows, LANES), 1)
+        mine_only = (lanes == node) | (lanes == node + node_count)
+        scale = jnp.sum(jnp.where(mine_only, scales, 0.0), axis=1, keepdims=True)
+        step = min(feat_out, 2 * LANES)
+        for start in range(0, feat_out, step):
+            result = jnp.dot(hidden, vd[:, start : start + step], preferred_element_type=F32)
+            scaled = (result.astype(BF16).astype(F32) * scale).reshape(PAIR, row_count, step)
+            ykeep[s, :, :, start : start + step] = scaled
+            ysend[s, :, :, start : start + step] = scaled.astype(BF16)
+        launch(remote(ysend.at[s, 1 - y], yrecv.at[s], y_send.at[s], y_recv.at[s], y_peer))
+
+    def give_back(s):
+        remote(ysend.at[s, 1 - y], yrecv.at[s], y_send.at[s], y_recv.at[s], y_peer).wait_recv()
+        total = ykeep[s, y] + yrecv[s].astype(F32)
+        if s == 0:
+            zown[...] = total
+        else:
+            zsend[s] = total.astype(BF16)
+            launch(remote(zsend.at[s], zrecv.at[z], z_send.at[s], z_recv.at[z], z_peers[s - 1]))
+
+    forward(1)
+    stages = (project, cross, activate, down, give_back)
+    for slot in range(groups + len(stages) - 1):
+        for delay, stage in enumerate(stages):
+            if 0 <= slot - delay < groups:
+                stage(slot - delay)
+            if delay == 0:
+                forward(slot + 2)
+
+    total = zown[...]
+    for s in range(1, groups):
+        origin = planes[s]
+        remote(
+            zsend.at[s], zrecv.at[origin], z_send.at[s], z_recv.at[origin], z_peers[s - 1]
+        ).wait_recv()
+        total = total + zrecv[origin].astype(F32)
+    out[...] = total.astype(BF16)
+    for copy in pending:
+        copy.wait_send()
+
+
+def fused_body(tokens, node_ids, mix_weights, w_gate, w_up, w_down):
+    row_count, feat = tokens.shape
+    node_count = lax.axis_size("node")
+    hid, feat_out = w_down.shape[1], w_down.shape[2]
+    groups, rows = node_count // PAIR, PAIR * row_count
+    half = hid // PAIR
+    quarters = PAIR * PAIR
+    anywhere = pl.BlockSpec(memory_space=pl.ANY)
+    vmem = pl.BlockSpec(memory_space=pltpu.VMEM)
+    dma = pltpu.SemaphoreType.DMA
+    return pl.pallas_call(
+        fused_kernel,
+        out_shape=jax.ShapeDtypeStruct((row_count, feat_out), BF16),
+        in_specs=[anywhere, vmem, vmem, anywhere, anywhere, anywhere],
+        out_specs=vmem,
+        scratch_shapes=[
+            pltpu.VMEM((node_count, row_count, feat + LANES), BF16),
+            pltpu.VMEM((feat, hid), BF16),
+            pltpu.VMEM((feat, hid), BF16),
+            pltpu.VMEM((hid, feat_out), BF16),
+            pltpu.VMEM((groups, rows, 2 * half), BF16),
+            pltpu.VMEM((groups, rows, 2 * half), BF16),
+            pltpu.VMEM((groups, rows, 2 * half), F32),
+            pltpu.VMEM((groups, rows, half), BF16),
+            pltpu.VMEM((groups, rows, half), BF16),
+            pltpu.VMEM((groups, quarters, rows, hid // quarters), BF16),
+            pltpu.VMEM((groups, PAIR, row_count, feat_out), BF16),
+            pltpu.VMEM((groups, PAIR, row_count, feat_out), F32),
+            pltpu.VMEM((groups, row_count, feat_out), BF16),
+            pltpu.VMEM((groups, row_count, feat_out), BF16),
+            pltpu.VMEM((groups, row_count, feat_out), BF16),
+            pltpu.VMEM((row_count, feat_out), F32),
+            dma((4,)),
+            dma((groups,)),
+            dma((groups,)),
+            dma((node_count,)),
+            dma((groups,)),
+            dma((groups,)),
+            dma((groups,)),
+            dma((groups,)),
+            dma((groups, quarters - 1)),
+            dma((groups, quarters)),
+            dma((groups,)),
+            dma((groups,)),
+            dma((groups,)),
+            dma((groups,)),
+        ],
+        compiler_params=pltpu.CompilerParams(
+            collective_id=0, has_side_effects=True, vmem_limit_bytes=40 * 1024 * 1024
+        ),
+        cost_estimate=pl.CostEstimate(
+            flops=2 * node_count * row_count * hid * (2 * feat + feat_out),
+            bytes_accessed=2 * hid * (2 * feat + feat_out),
+            transcendentals=node_count * row_count * hid // quarters,
+        ),
+    )(tokens, node_ids, mix_weights, w_gate, w_up, w_down)
+
+
+def slot_body(slot_cap, tokens, node_ids, mix_weights, w_gate, w_up, w_down):
     row_count, feat_width = tokens.shape
     pick_count = node_ids.shape[1]
     node_count = lax.axis_size("node")
-    slot_cap = max(2, 2 * row_count * pick_count // node_count)
     slot_total = node_count * slot_cap
     flat_ids = node_ids.reshape(-1)
     hit_table = (flat_ids[:, None] == jnp.arange(node_count, dtype=jnp.int32)[None, :]).astype(
@@ -45,6 +287,17 @@
         precision=lax.Precision.HIGHEST,
     )
     return mixed.astype(jnp.bfloat16)
+
+
+def body(tokens, node_ids, mix_weights, w_gate, w_up, w_down):
+    row_count, pick_count = node_ids.shape
+    node_count, local_count = lax.axis_size("node"), lax.axis_size("local")
+    slot_cap = max(2, 2 * row_count * pick_count // node_count)
+    args = (tokens, node_ids, mix_weights, w_gate, w_up, w_down)
+    whole_rows = slot_cap >= row_count and node_count % PAIR == 0 and 2 * node_count <= LANES
+    if whole_rows and local_count == PAIR * PAIR:
+        return fused_body(*args)
+    return slot_body(slot_cap, *args)
 
 
 def solution(mesh):

time: 102 us -> 46.1 us (0.45)
  waiting for transfers between devices: 49.5 us -> 0 us
  Pallas kernels: 0 us -> 38.1 us
  blocking collectives: 21.7 us -> 0 us
  between operations: 13.5 us -> 0.01 us
  matrix products: 8.79 us -> 0 us
  local copies, waits for them, and re-layouts: 1.21 us -> 7.77 us
  starting transfers between devices: 5.52 us -> 0 us
  other arithmetic: 1.31 us -> 0 us
    pallas_call x0 -> x1, Pallas kernels: none -> 38.1 us  [fused_body(): pl.pallas_call(fused_kernel, out_shape=jax.ShapeDtypeStruct((row_count, f...]
    psum x1 -> x0, waiting for transfers between devices: 35.4 us -> none  [body(): lax.psum(up_part.astype(jnp.bfloat16), 'local').astype(jnp.float32)]
    all_to_all x1 -> x0, blocking collectives: 21.7 us -> none  [body(): lax.all_to_all(outbound, 'node', split_axis=0, concat_axis=0, tiled=True)]
    all_to_all x1 -> x0, waiting for transfers between devices: 14.1 us -> none  [body(): lax.all_to_all(expert_out, 'node', split_axis=0, concat_axis=0, tiled=True)]
    dot_general x5 -> x0, matrix products: 8.79 us -> none  [the longest x1 3.57 us: body(): result = jnp.dot(active, w_down[0], preferred_element_type=jnp.float32)]
    unnamed x7 -> x11, local copies, waits for them, and re-layouts: 0.92 us -> 7.77 us
    all_to_all x1 -> x0, starting transfers between devices: 5.52 us -> none  [body(): lax.all_to_all(expert_out, 'node', split_axis=0, concat_axis=0, tiled=True)]
  transfers between devices with their start and end apart: 2 -> 0, of which waited for: 2 -> 0; matrix products, arithmetic and copies ran while one was open for 0% -> 0% of each run, Pallas kernels for 0% -> 0%
where the time goes in v1:
time: 46.1 us; the launch traced here: 45.8 us
  Pallas kernels  38.1 us (83%)
  local copies, waits for them, and re-layouts  7.77 us (17%)
    pallas_call x1, Pallas kernels, fused_body(): pl.pallas_call(fused_kernel, out_shape=jax.ShapeDtypeStruct((row_count, f...  38.1 us
    unnamed x11, local copies, waits for them, and re-layouts  7.77 us

profile of v1, /device:TPU:0, one launch (start us, length us, event | category | flops | bytes accessed | tf_op | source)
XLA Modules:
  0.0 45.8 jit_solution(12742611033185400719)
XLA Ops:
  0.0 0.8 %copy.7.ids = s32[32,4]{1,0:T(8,128)S(1)} copy(s32[32,4]{0,1:T(4,128)} %param.7) | data formatting | bytes 1024 | tf_op args[1]
  0.8 0.8 %copy.8.mix = f32[32,4]{1,0:T(8,128)S(1)} copy(f32[32,4]{0,1:T(4,128)} %param.8) | data formatting | bytes 1024 | tf_op args[2]
  1.5 0.0 copy-start
  1.5 1.6 %copy-done = bf16[1,1024,1024]{2,1,0:T(8,128)(2,1)S(1)} copy-done((bf16[1,1024,1024]{2,1,0:T(8,128)(2,1)S(1)}, bf16[1,1024,1024]{2,1,0:T(8,128)(2,1)}, u32[]{:S(2)}) %copy-start) | copy-done | bytes 2097176
  3.1 0.0 copy-start.1
  3.1 1.6 %copy-done.1 = bf16[1,1024,1024]{2,1,0:T(8,128)(2,1)S(1)} copy-done((bf16[1,1024,1024]{2,1,0:T(8,128)(2,1)S(1)}, bf16[1,1024,1024]{2,1,0:T(8,128)(2,1)}, u32[]{:S(2)}) %copy-start.1) | copy-done | bytes 2097176
  4.7 0.0 copy-start.2
  4.7 1.6 %copy-done.2 = bf16[1,1024,1024]{2,1,0:T(8,128)(2,1)S(1)} copy-done((bf16[1,1024,1024]{2,1,0:T(8,128)(2,1)S(1)}, bf16[1,1024,1024]{2,1,0:T(8,128)(2,1)}, u32[]{:S(2)}) %copy-start.2) | copy-done | bytes 2097176
  6.3 0.0 copy-start.3
  6.3 0.8 %copy-done.3 = bf16[32,1024]{1,0:T(8,128)(2,1)S(1)} copy-done((bf16[32,1024]{1,0:T(8,128)(2,1)S(1)}, bf16[32,1024]{1,0:T(8,128)(2,1)}, u32[]{:S(2)}) %copy-start.3) | copy-done | bytes 65560
  7.1 38.1 %shard_map.64 = bf16[32,1024]{1,0:T(8,128)(2,1)S(1)} custom-call(bf16[32,1024]{1,0:T(8,128)(2,1)S(1)} %copy-done.3, s32[32,4]{1,0:T(8,128)S(1)} %copy.7.ids, f32[32,4]{1,0:T(8,128)S(1)} %copy.8.mix, bf16[1,1024,1024]{2,1,0:T(8,128)(2,1)S(1)} %copy-done, bf16[1,1024,1024]{2,1,0:T(8,128)(2,1)S(1)} %copy-done.1, bf16[1,1024,1024]{2,1,0:T(8,128)(2,1)S(1)} %copy-done.2), custom_call_target="tpu_custom_call" | custom-call | flops 1610612736 | bytes 6291456 | tf_op jit(solution)/shard_map/pallas_call | solution.py:202
  45.2 0.6 %copy.10 = bf16[32,1024]{1,0:T(8,128)(2,1)} copy(bf16[32,1024]{1,0:T(8,128)(2,1)S(1)} %shard_map.64) | data formatting | bytes 131072
Async XLA Ops:
  1.5 1.6 %copy-start = (bf16[1,1024,1024]{2,1,0:T(8,128)(2,1)S(1)}, bf16[1,1024,1024]{2,1,0:T(8,128)(2,1)}, u32[]{:S(2)}) copy-start(bf16[1,1024,1024]{2,1,0:T(8,128)(2,1)} %wg.1) | copy-start | bytes 6291460
  3.1 1.6 %copy-start.1 = (bf16[1,1024,1024]{2,1,0:T(8,128)(2,1)S(1)}, bf16[1,1024,1024]{2,1,0:T(8,128)(2,1)}, u32[]{:S(2)}) copy-start(bf16[1,1024,1024]{2,1,0:T(8,128)(2,1)} %wu.1) | copy-start | bytes 6291460
  4.7 1.6 %copy-start.2 = (bf16[1,1024,1024]{2,1,0:T(8,128)(2,1)S(1)}, bf16[1,1024,1024]{2,1,0:T(8,128)(2,1)}, u32[]{:S(2)}) copy-start(bf16[1,1024,1024]{2,1,0:T(8,128)(2,1)} %wd.1) | copy-start | bytes 6291460
  6.3 0.8 %copy-start.3 = (bf16[32,1024]{1,0:T(8,128)(2,1)S(1)}, bf16[32,1024]{1,0:T(8,128)(2,1)}, u32[]{:S(2)}) copy-start(bf16[32,1024]{1,0:T(8,128)(2,1)} %tok.1) | copy-start | bytes 196612

commit v2 on v1

--- a/solution.py
+++ b/solution.py
@@ -9,6 +9,7 @@
 
 PAIR = 2
 LANES = 128
+VMEM_BYTES = 60 * 1024 * 1024
 F32 = jnp.float32
 BF16 = jnp.bfloat16
 
@@ -22,6 +23,11 @@
         result = result + (1 - digit if step & bit else digit) * bit
         bit *= 2
     return result
+
+
+def chunks_of(groups):
+    count = min(groups, 2)
+    return [list(range(first, groups, count))[::-1] for first in range(count)]
 
 
 def fused_kernel(
@@ -34,7 +40,7 @@
     node_count, row_count, wide = xbuf.shape
     feat = wide - LANES
     groups = node_count // PAIR
-    rows = PAIR * row_count
+    chunks = chunks_of(groups)
     hid = vg.shape[1]
     half, quarter = hid // PAIR, hid // (PAIR * PAIR)
     feat_out = vd.shape[1]
@@ -70,15 +76,21 @@
     for peer in peers:
         pl.semaphore_signal(barrier, inc=1, device_id=peer, device_id_type=pl.DeviceIdType.MESH)
 
-    lane = lax.broadcasted_iota(jnp.int32, (row_count, LANES), 1)
-    weight = jnp.zeros((row_count, LANES), F32)
-    for k in range(ids.shape[1]):
-        expert = ids[:, k : k + 1]
+    place = lax.broadcasted_iota(jnp.int32, (LANES, row_count), 0)
+    weight = jnp.zeros((LANES, row_count), F32)
+    for k in range(ids.shape[0]):
+        expert = ids[k : k + 1, :]
         weight += jnp.where(
-            (lane == expert) | (lane == expert + node_count), mix[:, k : k + 1], 0.0
+            (place == expert) | (place == expert + node_count), mix[k : k + 1, :], 0.0
         )
     head = weight.astype(BF16).astype(F32)
-    xbuf[node, :, feat:] = jnp.where(lane < node_count, head, weight - head).astype(BF16)
+    parts = jnp.where(place < node_count, head, weight - head).astype(BF16)
+    same = lax.broadcasted_iota(jnp.int32, (LANES, LANES), 0) == lax.broadcasted_iota(
+        jnp.int32, (LANES, LANES), 1
+    )
+    xbuf[node, :, feat:] = lax.dot_general(
+        parts, same.astype(BF16), (((0,), (0,)), ((), ())), preferred_element_type=F32
+    ).astype(BF16)
     loads[0].wait()
     pl.semaphore_wait(barrier, len(peers))
 
@@ -89,28 +101,30 @@
         pending.append(copy)
 
     launch(remote(xbuf.at[node], xbuf.at[node], a_ysend.at[0], a_recv.at[node], y_peer))
-    for s in range(1, groups):
+    for s in [s for chunk in chunks for s in chunk if s]:
         launch(
             remote(xbuf.at[node], xbuf.at[node], a_zsend.at[s], a_recv.at[node], z_peers[s - 1])
         )
 
     def forward(s):
-        if not 0 < s < groups:
-            return
         origin = planes[s] * PAIR + y
         copy = remote(xbuf.at[origin], xbuf.at[origin], a_ysend.at[s], a_recv.at[origin], y_peer)
         copy.wait_recv()
         launch(copy)
 
+    def blocks(s):
+        return [planes[step] * PAIR + side for side in range(PAIR) for step in chunks[s]]
+
     def project(s):
-        origin = planes[s] * PAIR + 1 - y
-        remote(
-            xbuf.at[origin], xbuf.at[origin], a_ysend.at[s], a_recv.at[origin], y_peer
-        ).wait_recv()
+        for step in chunks[s]:
+            origin = planes[step] * PAIR + 1 - y
+            remote(
+                xbuf.at[origin], xbuf.at[origin], a_ysend.at[step], a_recv.at[origin], y_peer
+            ).wait_recv()
         if s == 0:
             loads[1].wait()
             loads[2].wait()
-        inputs = xbuf[pl.ds(planes[s] * PAIR, PAIR), :, :feat].reshape(rows, feat)
+        inputs = jnp.concatenate([xbuf[origin, :, :feat] for origin in blocks(s)], axis=0)
         for target, first in ((psend, (1 - c) * half), (pown, c * half)):
             for part in range(PAIR):
                 cols = pl.ds(pl.multiple_of(first + part * quarter, quarter), quarter)
@@ -147,35 +161,56 @@
         if s == 0:
             loads[3].wait()
         hidden = jnp.concatenate([act[s, q] for q in range(PAIR * PAIR)], axis=1)
-        scales = xbuf[pl.ds(planes[s] * PAIR, PAIR), :, feat:].reshape(rows, LANES).astype(F32)
-        lanes = lax.broadcasted_iota(jnp.int32, (rows, LANES), 1)
+        scales = jnp.concatenate([xbuf[origin, :, feat:] for origin in blocks(s)], axis=0)
+        scales = scales.astype(F32)
+        lanes = lax.broadcasted_iota(jnp.int32, scales.shape, 1)
         mine_only = (lanes == node) | (lanes == node + node_count)
         scale = jnp.sum(jnp.where(mine_only, scales, 0.0), axis=1, keepdims=True)
-        step = min(feat_out, 2 * LANES)
-        for start in range(0, feat_out, step):
-            result = jnp.dot(hidden, vd[:, start : start + step], preferred_element_type=F32)
-            scaled = (result.astype(BF16).astype(F32) * scale).reshape(PAIR, row_count, step)
-            ykeep[s, :, :, start : start + step] = scaled
-            ysend[s, :, :, start : start + step] = scaled.astype(BF16)
-        launch(remote(ysend.at[s, 1 - y], yrecv.at[s], y_send.at[s], y_recv.at[s], y_peer))
+        width = min(feat_out, 2 * LANES)
+        for start in range(0, feat_out, width):
+            result = jnp.dot(hidden, vd[:, start : start + width], preferred_element_type=F32)
+            scaled = result.astype(BF16).astype(F32) * scale
+            scaled = scaled.reshape(PAIR, len(chunks[s]), row_count, width)
+            for k, step in enumerate(chunks[s]):
+                ykeep[step, :, :, start : start + width] = scaled[:, k]
+                ysend[step, :, :, start : start + width] = scaled[:, k].astype(BF16)
+        for step in chunks[s]:
+            launch(returning(step))
+
+    def returning(step):
+        return remote(
+            ysend.at[step, 1 - y], yrecv.at[step], y_send.at[step], y_recv.at[step], y_peer
+        )
 
     def give_back(s):
-        remote(ysend.at[s, 1 - y], yrecv.at[s], y_send.at[s], y_recv.at[s], y_peer).wait_recv()
-        total = ykeep[s, y] + yrecv[s].astype(F32)
-        if s == 0:
-            zown[...] = total
-        else:
-            zsend[s] = total.astype(BF16)
-            launch(remote(zsend.at[s], zrecv.at[z], z_send.at[s], z_recv.at[z], z_peers[s - 1]))
-
-    forward(1)
-    stages = (project, cross, activate, down, give_back)
-    for slot in range(groups + len(stages) - 1):
-        for delay, stage in enumerate(stages):
-            if 0 <= slot - delay < groups:
-                stage(slot - delay)
-            if delay == 0:
-                forward(slot + 2)
+        for step in chunks[s]:
+            returning(step).wait_recv()
+            total = ykeep[step, y] + yrecv[step].astype(F32)
+            if step == 0:
+                zown[...] = total
+            else:
+                zsend[step] = total.astype(BF16)
+                launch(
+                    remote(
+                        zsend.at[step], zrecv.at[z], z_send.at[step], z_recv.at[z],
+                        z_peers[step - 1],
+                    )
+                )
+
+    for s in range(len(chunks) + 2):
+        if s < len(chunks):
+            for step in chunks[s]:
+                if step:
+                    forward(step)
+            project(s)
+        if 0 < s <= len(chunks):
+            activate(s - 1)
+        if s < len(chunks):
+            cross(s)
+        if 0 < s <= len(chunks):
+            down(s - 1)
+        if s > 1:
+            give_back(s - 2)
 
     total = zown[...]
     for s in range(1, groups):
@@ -193,7 +228,9 @@
     row_count, feat = tokens.shape
     node_count = lax.axis_size("node")
     hid, feat_out = w_down.shape[1], w_down.shape[2]
-    groups, rows = node_count // PAIR, PAIR * row_count
+    groups = node_count // PAIR
+    cuts = chunks_of(groups)
+    count, rows = len(cuts), PAIR * row_count * len(cuts[0])
     half = hid // PAIR
     quarters = PAIR * PAIR
     anywhere = pl.BlockSpec(memory_space=pl.ANY)
@@ -209,12 +246,12 @@
             pltpu.VMEM((feat, hid), BF16),
             pltpu.VMEM((feat, hid), BF16),
             pltpu.VMEM((hid, feat_out), BF16),
-            pltpu.VMEM((groups, rows, 2 * half), BF16),
-            pltpu.VMEM((groups, rows, 2 * half), BF16),
-            pltpu.VMEM((groups, rows, 2 * half), F32),
-            pltpu.VMEM((groups, rows, half), BF16),
-            pltpu.VMEM((groups, rows, half), BF16),
-            pltpu.VMEM((groups, quarters, rows, hid // quarters), BF16),
+            pltpu.VMEM((count, rows, 2 * half), BF16),
+            pltpu.VMEM((count, rows, 2 * half), BF16),
+            pltpu.VMEM((count, rows, 2 * half), F32),
+            pltpu.VMEM((count, rows, half), BF16),
+            pltpu.VMEM((count, rows, half), BF16),
+            pltpu.VMEM((count, quarters, rows, hid // quarters), BF16),
             pltpu.VMEM((groups, PAIR, row_count, feat_out), BF16),
             pltpu.VMEM((groups, PAIR, row_count, feat_out), F32),
             pltpu.VMEM((groups, row_count, feat_out), BF16),
@@ -237,14 +274,14 @@
             dma((groups,)),
         ],
         compiler_params=pltpu.CompilerParams(
-            collective_id=0, has_side_effects=True, vmem_limit_bytes=40 * 1024 * 1024
+            collective_id=0, has_side_effects=True, vmem_limit_bytes=VMEM_BYTES
         ),
         cost_estimate=pl.CostEstimate(
             flops=2 * node_count * row_count * hid * (2 * feat + feat_out),
             bytes_accessed=2 * hid * (2 * feat + feat_out),
             transcendentals=node_count * row_count * hid // quarters,
         ),
-    )(tokens, node_ids, mix_weights, w_gate, w_up, w_down)
+    )(tokens, node_ids.T, mix_weights.T, w_gate, w_up, w_down)
 
 
 def slot_body(slot_cap, tokens, node_ids, mix_weights, w_gate, w_up, w_down):
@@ -294,7 +331,8 @@
     node_count, local_count = lax.axis_size("node"), lax.axis_size("local")
     slot_cap = max(2, 2 * row_count * pick_count // node_count)
     args = (tokens, node_ids, mix_weights, w_gate, w_up, w_down)
-    whole_rows = slot_cap >= row_count and node_count % PAIR == 0 and 2 * node_count <= LANES
+    paired = node_count % PAIR == 0 and (node_count // PAIR) % 2 == 0
+    whole_rows = slot_cap >= row_count and paired and 2 * node_count <= LANES
     if whole_rows and local_count == PAIR * PAIR:
         return fused_body(*args)
     return slot_body(slot_cap, *args)

time: 46.1 us -> 46.9 us (1.017)
  Pallas kernels: 38.1 us -> 45.2 us
  local copies, waits for them, and re-layouts: 7.77 us -> 1.47 us
    pallas_call x1, Pallas kernels: 38.1 us -> 45.2 us  [fused_body(): pl.pallas_call(fused_kernel, out_shape=jax.ShapeDtypeStruct((row_count, f...]
    unnamed x11 -> x1, local copies, waits for them, and re-layouts: 7.77 us -> 1.47 us
where the time goes in v2:
time: 46.9 us; the launch traced here: 46.7 us
  Pallas kernels  45.2 us (96%)
  local copies, waits for them, and re-layouts  1.47 us (3%)
    pallas_call x1, Pallas kernels, fused_body(): pl.pallas_call(fused_kernel, out_shape=jax.ShapeDtypeStruct((row_count, f...  45.2 us
    unnamed x1, local copies, waits for them, and re-layouts  1.47 us

profile of v2, /device:TPU:0, one launch (start us, length us, event | category | flops | bytes accessed | tf_op | source)
XLA Modules:
  0.0 46.7 jit_solution(9790502245905416550)
XLA Ops:
  0.0 45.2 %shard_map.64 = bf16[32,1024]{1,0:T(8,128)(2,1)} custom-call(bf16[32,1024]{1,0:T(8,128)(2,1)} %tok.1, s32[4,32]{1,0:T(4,128)} %bitcast.2, f32[4,32]{1,0:T(4,128)} %bitcast.3, bf16[1,1024,1024]{2,1,0:T(8,128)(2,1)} %wg.1, bf16[1,1024,1024]{2,1,0:T(8,128)(2,1)} %wu.1, bf16[1,1024,1024]{2,1,0:T(8,128)(2,1)} %wd.1), custom_call_target="tpu_custom_call" | custom-call | flops 1610612736 | bytes 6291456 | tf_op jit(solution)/shard_map/pallas_call | solution.py:239
  45.2 1.5 %copy.8 = bf16[32,1024]{1,0:T(8,128)(2,1)} copy(bf16[32,1024]{1,0:T(8,128)(2,1)} %shard_map.64) | data formatting | bytes 131072

commit v3 on v2

--- a/solution.py
+++ b/solution.py
@@ -26,8 +26,9 @@
 
 
 def chunks_of(groups):
-    count = min(groups, 2)
-    return [list(range(first, groups, count))[::-1] for first in range(count)]
+    middle = groups // 2
+    parts = [0], list(range(middle, 0, -1)), list(range(middle + 1, groups))
+    return [part for part in parts if part]
 
 
 def fused_kernel(
@@ -41,6 +42,7 @@
     feat = wide - LANES
     groups = node_count // PAIR
     chunks = chunks_of(groups)
+    sizes = [PAIR * row_count * len(chunk) for chunk in chunks]
     hid = vg.shape[1]
     half, quarter = hid // PAIR, hid // (PAIR * PAIR)
     feat_out = vd.shape[1]
@@ -69,8 +71,7 @@
         pltpu.make_async_copy(wu.at[0], vu, load_sem.at[2]),
         pltpu.make_async_copy(wd.at[0], vd, load_sem.at[3]),
     ]
-    for load in loads:
-        load.start()
+    loads[0].start()
     barrier = pltpu.get_barrier_semaphore()
     peers = [y_peer, c_peer, x_peer, d_peer] + z_peers
     for peer in peers:
@@ -92,6 +93,8 @@
         parts, same.astype(BF16), (((0,), (0,)), ((), ())), preferred_element_type=F32
     ).astype(BF16)
     loads[0].wait()
+    loads[1].start()
+    loads[2].start()
     pl.semaphore_wait(barrier, len(peers))
 
     pending = []
@@ -105,6 +108,21 @@
         launch(
             remote(xbuf.at[node], xbuf.at[node], a_zsend.at[s], a_recv.at[node], z_peers[s - 1])
         )
+
+    loads[3].start()
+
+    def span(ref, s):
+        return ref.at[s, pl.ds(0, sizes[s])]
+
+    def to_core(s):
+        return remote(span(psend, s), span(precv, s), p_send.at[s], p_recv.at[s], c_peer)
+
+    def to_chip(s):
+        return remote(span(xsend, s), span(xrecv, s), x_send.at[s], x_recv.at[s], x_peer)
+
+    def share(s, k, slot, peer):
+        block = act.at[s, slot, pl.ds(0, sizes[s])]
+        return remote(block, block, t_send.at[s, k], t_recv.at[s, slot], peer)
 
     def forward(s):
         origin = planes[s] * PAIR + y
@@ -131,36 +149,33 @@
                 for which, matrix in enumerate((vg, vu)):
                     product = jnp.dot(inputs, matrix[:, cols], preferred_element_type=F32)
                     start = (part * 2 + which) * quarter
-                    target[s, :, start : start + quarter] = product.astype(target.dtype)
+                    target[s, : sizes[s], start : start + quarter] = product.astype(target.dtype)
             if target is psend:
-                launch(remote(psend.at[s], precv.at[s], p_send.at[s], p_recv.at[s], c_peer))
+                launch(to_core(s))
 
     def cross(s):
-        remote(psend.at[s], precv.at[s], p_send.at[s], p_recv.at[s], c_peer).wait_recv()
+        to_core(s).wait_recv()
+        n = sizes[s]
         cols = pl.ds(pl.multiple_of((1 - x) * 2 * quarter, 2 * quarter), 2 * quarter)
-        xsend[s] = (pown[s, :, cols] + precv[s, :, cols].astype(F32)).astype(BF16)
-        launch(remote(xsend.at[s], xrecv.at[s], x_send.at[s], x_recv.at[s], x_peer))
+        xsend[s, :n] = (pown[s, :n, cols] + precv[s, :n, cols].astype(F32)).astype(BF16)
+        launch(to_chip(s))
 
     def activate(s):
-        remote(xsend.at[s], xrecv.at[s], x_send.at[s], x_recv.at[s], x_peer).wait_recv()
+        to_chip(s).wait_recv()
+        n = sizes[s]
         cols = pl.ds(pl.multiple_of(x * 2 * quarter, 2 * quarter), 2 * quarter)
-        total = pown[s, :, cols] + precv[s, :, cols].astype(F32) + xrecv[s].astype(F32)
+        total = pown[s, :n, cols] + precv[s, :n, cols].astype(F32) + xrecv[s, :n].astype(F32)
         gate, up = total[:, :quarter], total[:, quarter:]
-        act[s, mine] = (gate / (1.0 + jnp.exp(-gate)) * up).astype(BF16)
+        act[s, mine, :n] = (gate / (1.0 + jnp.exp(-gate)) * up).astype(BF16)
         for k, peer in enumerate((d_peer, x_peer, c_peer)):
-            launch(
-                remote(act.at[s, mine], act.at[s, mine], t_send.at[s, k], t_recv.at[s, mine], peer)
-            )
+            launch(share(s, k, mine, peer))
 
     def down(s):
         for k, (cc, xx) in enumerate(((1 - c, 1 - x), (c, 1 - x), (1 - c, x))):
-            slot = cc * PAIR + xx
-            remote(
-                act.at[s, slot], act.at[s, slot], t_send.at[s, k], t_recv.at[s, slot], d_peer
-            ).wait_recv()
+            share(s, k, cc * PAIR + xx, d_peer).wait_recv()
         if s == 0:
             loads[3].wait()
-        hidden = jnp.concatenate([act[s, q] for q in range(PAIR * PAIR)], axis=1)
+        hidden = jnp.concatenate([act[s, q, : sizes[s]] for q in range(PAIR * PAIR)], axis=1)
         scales = jnp.concatenate([xbuf[origin, :, feat:] for origin in blocks(s)], axis=0)
         scales = scales.astype(F32)
         lanes = lax.broadcasted_iota(jnp.int32, scales.shape, 1)
@@ -197,20 +212,28 @@
                     )
                 )
 
-    for s in range(len(chunks) + 2):
-        if s < len(chunks):
-            for step in chunks[s]:
-                if step:
-                    forward(step)
-            project(s)
-        if 0 < s <= len(chunks):
+    project(0)
+    cross(0)
+    for chunk in chunks[1:]:
+        for step in chunk:
+            forward(step)
+    activate(0)
+    for s in range(1, len(chunks)):
+        project(s)
+        if s > 1:
             activate(s - 1)
-        if s < len(chunks):
-            cross(s)
-        if 0 < s <= len(chunks):
-            down(s - 1)
-        if s > 1:
-            give_back(s - 2)
+        cross(s)
+    down(0)
+    give_back(0)
+    last = len(chunks) - 1
+    for s in range(1, last):
+        down(s)
+    if last > 0:
+        activate(last)
+        for s in range(1, last):
+            give_back(s)
+        down(last)
+        give_back(last)
 
     total = zown[...]
     for s in range(1, groups):
@@ -230,7 +253,7 @@
     hid, feat_out = w_down.shape[1], w_down.shape[2]
     groups = node_count // PAIR
     cuts = chunks_of(groups)
-    count, rows = len(cuts), PAIR * row_count * len(cuts[0])
+    count, rows = len(cuts), PAIR * row_count * max(len(cut) for cut in cuts)
     half = hid // PAIR
     quarters = PAIR * PAIR
     anywhere = pl.BlockSpec(memory_space=pl.ANY)

time: 46.9 us -> 43.5 us (0.928)
  Pallas kernels: 45.2 us -> 41.8 us
    pallas_call x1, Pallas kernels: 45.2 us -> 41.8 us  [fused_body(): pl.pallas_call(fused_kernel, out_shape=jax.ShapeDtypeStruct((row_count, f...]
where the time goes in v3:
time: 43.5 us; the launch traced here: 43.2 us
  Pallas kernels  41.8 us (96%)
  local copies, waits for them, and re-layouts  1.47 us (3%)
    pallas_call x1, Pallas kernels, fused_body(): pl.pallas_call(fused_kernel, out_shape=jax.ShapeDtypeStruct((row_count, f...  41.8 us
    unnamed x1, local copies, waits for them, and re-layouts  1.47 us

profile of v3, /device:TPU:0, one launch (start us, length us, event | category | flops | bytes accessed | tf_op | source)
XLA Modules:
  0.0 43.2 jit_solution(17280656770851752540)
XLA Ops:
  0.0 41.8 %shard_map.64 = bf16[32,1024]{1,0:T(8,128)(2,1)} custom-call(bf16[32,1024]{1,0:T(8,128)(2,1)} %tok.1, s32[4,32]{1,0:T(4,128)} %bitcast.2, f32[4,32]{1,0:T(4,128)} %bitcast.3, bf16[1,1024,1024]{2,1,0:T(8,128)(2,1)} %wg.1, bf16[1,1024,1024]{2,1,0:T(8,128)(2,1)} %wu.1, bf16[1,1024,1024]{2,1,0:T(8,128)(2,1)} %wd.1), custom_call_target="tpu_custom_call" | custom-call | flops 1610612736 | bytes 6291456 | tf_op jit(solution)/shard_map/pallas_call | solution.py:262
  41.8 1.5 %copy.8 = bf16[32,1024]{1,0:T(8,128)(2,1)} copy(bf16[32,1024]{1,0:T(8,128)(2,1)} %shard_map.64) | data formatting | bytes 131072

commit v4 on v3

--- a/solution.py
+++ b/solution.py
@@ -26,9 +26,7 @@
 
 
 def chunks_of(groups):
-    middle = groups // 2
-    parts = [0], list(range(middle, 0, -1)), list(range(middle + 1, groups))
-    return [part for part in parts if part]
+    return [[step] for step in range(groups)]
 
 
 def fused_kernel(
@@ -212,28 +210,15 @@
                     )
                 )
 
-    project(0)
-    cross(0)
-    for chunk in chunks[1:]:
-        for step in chunk:
-            forward(step)
-    activate(0)
-    for s in range(1, len(chunks)):
-        project(s)
-        if s > 1:
-            activate(s - 1)
-        cross(s)
-    down(0)
-    give_back(0)
-    last = len(chunks) - 1
-    for s in range(1, last):
-        down(s)
-    if last > 0:
-        activate(last)
-        for s in range(1, last):
-            give_back(s)
-        down(last)
-        give_back(last)
+    if groups > 1:
+        forward(1)
+    stages = (project, cross, activate, down, give_back)
+    for slot in range(groups + len(stages) - 1):
+        for delay, stage in enumerate(stages):
+            if 0 <= slot - delay < groups:
+                stage(slot - delay)
+            if delay == 0 and slot + 2 < groups:
+                forward(slot + 2)
 
     total = zown[...]
     for s in range(1, groups):

time: 43.5 us -> 40.6 us (0.933)
  Pallas kernels: 41.8 us -> 38.9 us
    pallas_call x1, Pallas kernels: 41.8 us -> 38.9 us  [fused_body(): pl.pallas_call(fused_kernel, out_shape=jax.ShapeDtypeStruct((row_count, f...]
where the time goes in v4:
time: 40.6 us; the launch traced here: 40.4 us
  Pallas kernels  38.9 us (96%)
  local copies, waits for them, and re-layouts  1.47 us (4%)
    pallas_call x1, Pallas kernels, fused_body(): pl.pallas_call(fused_kernel, out_shape=jax.ShapeDtypeStruct((row_count, f...  38.9 us
    unnamed x1, local copies, waits for them, and re-layouts  1.47 us

profile of v4, /device:TPU:0, one launch (start us, length us, event | category | flops | bytes accessed | tf_op | source)
XLA Modules:
  0.0 40.4 jit_solution(16856303688694823127)
XLA Ops:
  0.0 38.9 %shard_map.64 = bf16[32,1024]{1,0:T(8,128)(2,1)} custom-call(bf16[32,1024]{1,0:T(8,128)(2,1)} %tok.1, s32[4,32]{1,0:T(4,128)} %bitcast.2, f32[4,32]{1,0:T(4,128)} %bitcast.3, bf16[1,1024,1024]{2,1,0:T(8,128)(2,1)} %wg.1, bf16[1,1024,1024]{2,1,0:T(8,128)(2,1)} %wu.1, bf16[1,1024,1024]{2,1,0:T(8,128)(2,1)} %wd.1), custom_call_target="tpu_custom_call" | custom-call | flops 1610612736 | bytes 6291456 | tf_op jit(solution)/shard_map/pallas_call | solution.py:247
  38.9 1.5 %copy.8 = bf16[32,1024]{1,0:T(8,128)(2,1)} copy(bf16[32,1024]{1,0:T(8,128)(2,1)} %shard_map.64) | data formatting | bytes 131072
